TPU v7x, 128 devices: a whole 4x4x4 slice. The times are simulated.
128 devices in a mesh: grp: 16 (over x_lo, y, core), blk: 8 (over x_hi, z).
Axes of the slice: x: 4 (x_hi: 2, x_lo: 2; x = x_hi * 2 + x_lo), y: 4, z: 4, core: 2. Of those that a mesh axis runs over, the one named last changes fastest.
Arguments:
- embed: bfloat16 [65536, 1024], P(('grp', 'blk')), may hold values from -6 to 6
- dest: int32 [65536], P(('grp', 'blk')), may hold values from 0 to 127, as said below
- slot: int32 [65536], P(('grp', 'blk')), may hold values from 0 to 511, as said below
Outputs:
- best: float32 [65536], P(('grp', 'blk'))
Inputs may be any that keep to these rules, and one draw needn't show every extreme that they name: Each device index receives exactly 512 documents; at most 8 documents of one device's rows name the same dest, and in every draw some device sends exactly 8 to some dest. The pairs (dest, slot) are all different.
All inputs are finite; a program needn't handle non-finite values.
Results may differ from a plain program's by a relative error of at most 0.0013.
Values may be sent and summed in bfloat16 or wider, within the bound.
A program may use at most 64 MiB of HBM per device.

v0:
```python
import jax
import jax.numpy as jnp
from jax import lax
from jax.sharding import PartitionSpec as P


def tile_scores(left, right):
    return lax.dot_general(
        left, right, (((1,), (1,)), ((), ())), preferred_element_type=jnp.float32
    )


def on_device(embed, dest, slot):
    count = embed.shape[0]
    width = embed.shape[1]
    ndev = lax.axis_size(("grp", "blk"))
    cap = 2 * count // ndev
    onehot = (dest[:, None] == jnp.arange(ndev, dtype=jnp.int32)[None, :]).astype(jnp.bfloat16)
    lower = (
        lax.broadcasted_iota(jnp.int32, (count, count), 0)
        > lax.broadcasted_iota(jnp.int32, (count, count), 1)
    ).astype(jnp.bfloat16)
    before = jnp.dot(lower, onehot, preferred_element_type=jnp.float32)
    rank = jnp.sum(before * onehot.astype(jnp.float32), axis=1).astype(jnp.int32)
    position = dest * cap + rank
    send_rows = (
        jnp.zeros((ndev * cap, width), jnp.bfloat16)
        .at[position]
        .set(embed)
        .reshape(ndev, cap, width)
    )
    send_slots = jnp.full((ndev * cap,), count, jnp.int32).at[position].set(slot).reshape(ndev, cap)
    arrived = lax.all_to_all(send_rows, ("grp", "blk"), split_axis=0, concat_axis=0, tiled=True)
    arrived_slots = lax.all_to_all(
        send_slots, ("grp", "blk"), split_axis=0, concat_axis=0, tiled=True
    ).reshape(-1)
    members = (
        jnp.zeros((count, width), jnp.bfloat16)
        .at[arrived_slots]
        .set(arrived.reshape(-1, width), mode="drop")
    )
    wide = members.astype(jnp.float32)
    unit = (wide * lax.rsqrt(jnp.sum(wide * wide, axis=1, keepdims=True) + 1e-06)).astype(
        jnp.bfloat16
    )
    my_start = lax.axis_index("blk") * count
    row_ids = my_start + jnp.arange(count, dtype=jnp.int32)
    piece = lax.all_gather(unit, "blk", axis=0, tiled=True)
    scores = tile_scores(unit, piece)
    col_ids = jnp.arange(piece.shape[0], dtype=jnp.int32)
    scores = jnp.where(row_ids[:, None] == col_ids[None, :], jnp.float32(-3.0), scores)
    best_member = jnp.maximum(jnp.full((count,), -3.0, jnp.float32), jnp.max(scores, axis=1))
    reply = best_member.at[arrived_slots].get(mode="fill", fill_value=0.0).reshape(ndev, cap)
    returned_best = lax.all_to_all(
        reply, ("grp", "blk"), split_axis=0, concat_axis=0, tiled=True
    ).reshape(-1)
    return returned_best[position]


def solution(mesh):
    placed = (P(("grp", "blk"), None), P(("grp", "blk")), P(("grp", "blk")))
    return jax.shard_map(
        on_device, mesh=mesh, in_specs=placed, out_specs=P(("grp", "blk")), check_vma=False
    )
```

profile of v0, /device:TPU:1, one launch (start us, length us, event | category | flops | bytes accessed | tf_op | source)
XLA Modules:
  0.0 221.6 jit_solution(5052692268056563203)
XLA Ops:
  6.5 1.1 fusion.4
  7.6 0.7 compare_select_fusion.2
  8.3 2.6 %scatter_custom_fusion = s32[1024]{0:T(1024)S(1)} fusion(s32[512]{0:T(512)S(1)} %compare_select_fusion.2, s32[512]{0:T(512)} %param.5, s32[]{:T(128)} %constant.11.clone.1), kind=kCustom, calls=%fused_computation.30 | custom fusion | bytes 4608 | tf_op jit(solution)/shard_map/scatter | solution.py:32
  10.9 0.7 all_to_all.13
  11.6 11.5 %all-to-all-start = ((s32[128,1,8]{2,1,0:T(1,128)}), s32[128,1,8]{2,1,0:T(1,128)S(1)}, u32[]{:S(2)}, u32[]{:S(2)}) async-start(s32[128,1,8]{2,1,0:T(1,128)} %bitcast), calls=%async_computation | async-start | bytes 131072 | tf_op jit(solution)/shard_map/all_to_all | solution.py:34
  23.1 4.8 %scatter_custom_fusion.1 = bf16[1024,1024]{1,0:T(8,128)(2,1)} fusion(s32[512]{0:T(512)S(1)} %compare_select_fusion.2, bf16[512,1024]{1,0:T(8,128)(2,1)} %param.3, bf16[]{:T(256)} %constant.1.clone.1), kind=kCustom, calls=%fused_computation.15 | custom fusion | bytes 2097664 | tf_op jit(solution)/shard_map/scatter | solution.py:29
  27.9 4.5 %all-to-all-done = s32[128,1,8]{2,1,0:T(1,128)S(1)} async-done(((s32[128,1,8]{2,1,0:T(1,128)}), s32[128,1,8]{2,1,0:T(1,128)S(1)}, u32[]{:S(2)}, u32[]{:S(2)}) %all-to-all-start) | async-done | bytes 4128 | tf_op jit(solution)/shard_map/all_to_all | solution.py:34
  32.4 5.3 %all-to-all-start.1 = ((bf16[128,8,1024]{2,1,0:T(8,128)(2,1)}), bf16[128,8,1024]{2,1,0:T(8,128)(2,1)S(1)}, u32[]{:S(2)}, u32[]{:S(2)}) async-start(bf16[128,8,1024]{2,1,0:T(8,128)(2,1)} %bitcast.12), calls=%async_computation.1 | async-start | bytes 4194304 | tf_op jit(solution)/shard_map/all_to_all | solution.py:33
  37.8 0.5 broadcast.91
  38.3 0.8 reduce.6
  39.1 0.1 reshape.68
  39.2 27.0 %all-to-all-done.1 = bf16[128,8,1024]{2,1,0:T(8,128)(2,1)S(1)} async-done(((bf16[128,8,1024]{2,1,0:T(8,128)(2,1)}), bf16[128,8,1024]{2,1,0:T(8,128)(2,1)S(1)}, u32[]{:S(2)}, u32[]{:S(2)}) %all-to-all-start.1) | async-done | bytes 2097184 | tf_op jit(solution)/shard_map/all_to_all | solution.py:33
  66.2 5.7 %scatter_custom_fusion.2 = bf16[512,1024]{1,0:T(8,128)(2,1)S(1)} fusion(s32[1024]{0:T(1024)S(1)} %bitcast.14, bf16[128,8,1024]{2,1,0:T(8,128)(2,1)S(1)} %all-to-all-done.1, bf16[]{:T(256)} %constant.1.clone.1), kind=kCustom, calls=%fused_computation.11 | custom fusion | bytes 3145730 | tf_op jit(solution)/shard_map/scatter | solution.py:40
  71.9 0.3 fusion
  72.2 1.3 fusion.1
  73.5 104.6 %all-gather.2.cloned.1.call-done = bf16[4096,1024]{1,0:T(8,128)(2,1)} async-done(((bf16[512,1024]{1,0:T(8,128)(2,1)}), bf16[4096,1024]{1,0:T(8,128)(2,1)}) %all-gather.2.cloned.1.call-update) | async-done | bytes 8388624 | tf_op jit(solution)/shard_map/all_gather | solution.py:48
  178.1 8.4 %select_reduce_fusion = f32[512]{0:T(512)S(1)} fusion(bf16[512,1024]{1,0:T(8,128)(2,1)} %fusion.1, bf16[4096,1024]{1,0:T(8,128)(2,1)} %all-gather.2.cloned.1.call-done, s32[512]{0:T(512)S(1)} %iota_add_fusion), kind=kOutput, calls=%fused_computation.5 | convolution fusion | flops 4301258240 | bytes 9441280 | tf_op jit(solution)/shard_map/dot_general | solution.py:8
  186.5 6.9 %gather_fusion = f32[1024]{0:T(1024)S(1)} fusion(f32[512]{0:T(512)S(1)} %broadcast_maximum_fusion, s32[1024]{0:T(1024)S(1)} %broadcast_clamp_fusion), kind=kCustom, calls=%fused_computation | custom fusion | bytes 12288 | tf_op jit(solution)/shard_map/gather | solution.py:53
  193.5 0.6 and_select_fusion
  194.1 6.5 %all-to-all-start.2 = ((f32[128,1,8]{2,1,0:T(1,128)}), f32[128,1,8]{2,1,0:T(1,128)S(1)}, u32[]{:S(2)}, u32[]{:S(2)}) async-start(f32[128,1,8]{2,1,0:T(1,128)} %bitcast.7), calls=%async_computation.2 | async-start | bytes 131072 | tf_op jit(solution)/shard_map/all_to_all | solution.py:54
  200.6 9.3 %all-to-all-done.2 = f32[128,1,8]{2,1,0:T(1,128)S(1)} async-done(((f32[128,1,8]{2,1,0:T(1,128)}), f32[128,1,8]{2,1,0:T(1,128)S(1)}, u32[]{:S(2)}, u32[]{:S(2)}) %all-to-all-start.2) | async-done | bytes 4128 | tf_op jit(solution)/shard_map/all_to_all | solution.py:54
  209.9 0.5 broadcast.92
  210.4 0.8 reduce.7
  211.3 3.4 %gather_fusion.1 = f32[512]{0:T(512)} fusion(f32[1024]{0:T(1024)S(1)} %reshape.71, s32[1024]{0:T(1024)S(1)} %pad_clamp_fusion), kind=kCustom, calls=%fused_computation.1 | custom fusion | bytes 6144 | tf_op jit(solution)/shard_map/gather | solution.py:57
  (10 shorter events, 0.3 us)
Async XLA Ops:
  11.6 20.8 %all-to-all-start = ((s32[128,1,8]{2,1,0:T(1,128)}), s32[128,1,8]{2,1,0:T(1,128)S(1)}, u32[]{:S(2)}, u32[]{:S(2)}) async-start(s32[128,1,8]{2,1,0:T(1,128)} %bitcast), calls=%async_computation | async-start | bytes 131072 | tf_op jit(solution)/shard_map/all_to_all | solution.py:34
  32.4 33.8 %all-to-all-start.1 = ((bf16[128,8,1024]{2,1,0:T(8,128)(2,1)}), bf16[128,8,1024]{2,1,0:T(8,128)(2,1)S(1)}, u32[]{:S(2)}, u32[]{:S(2)}) async-start(bf16[128,8,1024]{2,1,0:T(8,128)(2,1)} %bitcast.12), calls=%async_computation.1 | async-start | bytes 4194304 | tf_op jit(solution)/shard_map/all_to_all | solution.py:33
  37.7 140.4 %all-gather.2.cloned.1.call-start = ((), (), s32[]{:S(2)}) async-start(), calls=%async_computation.3 | async-start | bytes 9437184 | tf_op jit(solution)/shard_map/all_gather | solution.py:48
  194.1 15.8 %all-to-all-start.2 = ((f32[128,1,8]{2,1,0:T(1,128)}), f32[128,1,8]{2,1,0:T(1,128)S(1)}, u32[]{:S(2)}, u32[]{:S(2)}) async-start(f32[128,1,8]{2,1,0:T(1,128)} %bitcast.7), calls=%async_computation.2 | async-start | bytes 131072 | tf_op jit(solution)/shard_map/all_to_all | solution.py:54
Sparse Core Ops, SparseCore 0:
  73.6 104.4 all-gather.1
where the time goes:
time: 222 us
  waiting for transfers between devices  145 us (65%)
  local copies, waits for them, and re-layouts  25.4 us (11%)
  starting transfers between devices  23.3 us (10%)
  between operations  13.5 us (6%)
  matrix products  9.47 us (4%)
  other arithmetic  4.57 us (2%)
    all_gather x1, waiting for transfers between devices, on_device(): piece = lax.all_gather(unit, 'blk', axis=0, tiled=True)  105 us
    all_to_all x1, waiting for transfers between devices, on_device(): lax.all_to_all(send_rows, ('grp', 'blk'), split_axis=0, concat_axis=0, ti...  27 us
    all_to_all x1, starting transfers between devices, on_device(): lax.all_to_all(send_slots, ('grp', 'blk'), split_axis=0, concat_axis=0, t...  11.5 us
    all_to_all x1, waiting for transfers between devices, on_device(): lax.all_to_all(reply, ('grp', 'blk'), split_axis=0, concat_axis=0, tiled=...  9.31 us
    dot_general x1, matrix products, tile_scores(): lax.dot_general(left, right, (((1,), (1,)), ((), ())), preferred_element_...  8.41 us
    gather x2, local copies, waits for them, and re-layouts, on_device(): best_member.at[arrived_slots].get(mode='fill', fill_value=0.0)  6.94 us
    all_to_all x1, starting transfers between devices, on_device(): lax.all_to_all(reply, ('grp', 'blk'), split_axis=0, concat_axis=0, tiled=...  6.46 us
    scatter x1, local copies, waits for them, and re-layouts, on_device(): members = jnp.zeros((count, width), jnp.bfloat16).at[arrived_slots].set(a...  5.67 us
  transfers between devices with their start and end apart: 4, of which 4 were waited for; matrix products, arithmetic and copies ran while one was open for 3% of the time, Pallas kernels for 0%

commit v1 on v0

v1 whole, which is shorter than its diff:
```python
import jax
import jax.numpy as jnp
from jax import lax
from jax.experimental import pallas as pl
from jax.experimental.pallas import tpu as pltpu
from jax.sharding import PartitionSpec as P

MESH = pl.DeviceIdType.MESH
GROUP = 64
N_MSG = 16
ROWS = GROUP * N_MSG
HALF = ROWS // 2
MARK = 4.0
LOW = -8.0

ORDER = [
    (0, 0, 0), (0, 2, 1), (1, 2, 1), (0, 1, 1), (1, 3, 1), (0, 3, 1), (1, 1, 1), (0, 2, 0),
    (1, 2, 0), (0, 1, 0), (1, 3, 0), (0, 3, 0), (1, 1, 0), (0, 0, 1), (1, 0, 1), (1, 0, 0),
]


def slot_of(s, d, f):
    return (d * 2 + f) * 2 + s


def place():
    g = lax.axis_index("grp")
    b = lax.axis_index("blk")
    x = (b // 4) * 2 + g // 8
    y = (g // 2) % 4
    z = b % 4
    c = g % 2
    return x, y, z, c


def device(x, y, z, c):
    return ((x % 2) * 8 + y * 2 + c, (x // 2) * 4 + z)


def flip(y, kind):
    low = y % 2
    return jnp.where(kind == 0, 3 - y, y + 1 - 2 * low)


def mate(y, kind):
    return flip(y, 1 - kind)


def routed(x, y, z, c, s, d, f, sign):
    here = c if s == 0 else 1 - c
    kind = here if sign == 1 else c
    step = (4 + sign * d) % 4
    yy = flip(y, kind) if f else y
    xx = jnp.where(kind == 0, lax.rem(x + step, 4), x)
    zz = jnp.where(kind == 0, z, lax.rem(z + step, 4))
    return device(xx, yy, zz, here)


def ring(x, y, z, c, step, paired):
    yy = mate(y, c) if paired else y
    xx = jnp.where(c == 0, x, lax.rem(x + step, 4))
    zz = jnp.where(c == 0, lax.rem(z + step, 4), z)
    return device(xx, yy, zz, c)


def nt(a, b):
    return lax.dot_general(a, b, (((1,), (1,)), ((), ())), preferred_element_type=jnp.float32)


def kernel(
    embed_ref, dest_ref, out_ref,
    unit, pack, blk_b, blk_a, blk_c, blk_e, low_b, low_a, low_c, low_e,
    max_b, max_a, max_c, max_e, got, table,
    pack_send, pack_recv, up_send, up_recv, down_send, down_recv, pair_send, pair_recv,
    part_send, part_recv, reply_send, reply_recv, self_sem,
):
    x, y, z, c = place()
    r = jnp.where(c == 0, z, x)
    wrapped = jnp.where(r >= 2, 1, 0)
    odd = y % 2

    barrier = pltpu.get_barrier_semaphore()
    partners = []
    for s, d, f in ORDER[1:]:
        partners.append(routed(x, y, z, c, s, d, f, -1))
    for s, d, f in ORDER[1:]:
        if s == 1 and (d, f) != (0, 0):
            partners.append(routed(x, y, z, c, s, d, f, 1))
    up = ring(x, y, z, c, 1, False)
    down = ring(x, y, z, c, 3, False)
    across = ring(x, y, z, c, 0, True)
    up_across = ring(x, y, z, c, 1, True)
    down_across = ring(x, y, z, c, 3, True)
    partners += [up, down, across, down_across]
    for other in partners:
        pl.semaphore_signal(barrier, inc=1, device_id=other, device_id_type=MESH)

    wide = embed_ref[...].astype(jnp.float32)
    scale = lax.rsqrt(jnp.sum(wide * wide, axis=1, keepdims=True) + 1e-06)
    unit[...] = (wide * scale).astype(jnp.bfloat16)

    dest = dest_ref[...]
    count = dest.shape[1]
    cluster = dest // 8
    kind = cluster // 8
    ring_at = (cluster // 2) % 4
    pair_at = cluster % 2
    s_of = jnp.where(kind == c, 0, 1)
    d_of = jnp.where(kind == 0, ring_at + 4 - x, ring_at + 4 - z) % 4
    my_pair0 = y // 2
    my_pair1 = ((y + 1) % 4) // 2
    f_of = jnp.where(jnp.where(kind == 0, my_pair0, my_pair1) == pair_at, 0, 1)
    code = (d_of * 2 + f_of) * 2 + s_of
    message = jnp.zeros_like(code)
    for j, (s, d, f) in enumerate(ORDER):
        message = jnp.where(code == slot_of(s, d, f), j, message)
    mine = lax.broadcasted_iota(jnp.int32, (N_MSG, count), 0) == message
    earlier = (
        lax.broadcasted_iota(jnp.int32, (count, count), 0)
        < lax.broadcasted_iota(jnp.int32, (count, count), 1)
    ).astype(jnp.float32).astype(jnp.bfloat16)
    mine_f = mine.astype(jnp.float32)
    before = jnp.dot(mine_f.astype(jnp.bfloat16), earlier, preferred_element_type=jnp.float32)
    rank = jnp.sum(before * mine_f, axis=0, keepdims=True).astype(jnp.int32)
    position = message * GROUP + rank

    def send(j):
        s, d, f = ORDER[j]
        rows = pl.ds(slot_of(s, d, f) * GROUP, GROUP)
        return pltpu.make_async_remote_copy(
            src_ref=pack.at[pl.ds(j * GROUP, GROUP)], dst_ref=blk_b.at[rows],
            send_sem=pack_send.at[j], recv_sem=pack_recv.at[j],
            device_id=routed(x, y, z, c, s, d, f, 1), device_id_type=MESH,
        )

    def spread(j, upward):
        rows = pl.ds(slot_of(*ORDER[j]) * GROUP, GROUP)
        return pltpu.make_async_remote_copy(
            src_ref=blk_b.at[rows], dst_ref=(blk_a if upward else blk_c).at[rows],
            send_sem=(up_send if upward else down_send).at[j],
            recv_sem=(up_recv if upward else down_recv).at[j],
            device_id=up if upward else down, device_id_type=MESH,
        )

    def relay(j):
        rows = pl.ds(slot_of(*ORDER[j]) * GROUP, GROUP)
        return pltpu.make_async_remote_copy(
            src_ref=blk_c.at[rows], dst_ref=blk_e.at[rows],
            send_sem=pair_send.at[j], recv_sem=pair_recv.at[j],
            device_id=across, device_id_type=MESH,
        )

    part = 4
    size = ROWS // part
    for k in range(part):
        at = lax.broadcasted_iota(jnp.int32, (size, count), 0) + k * size
        pick = (at == position).astype(jnp.float32)
        rows = jnp.dot(pick.astype(jnp.bfloat16), unit[...], preferred_element_type=jnp.float32)
        empty = jnp.sum(pick, axis=1, keepdims=True) < 0.5
        lane = lax.broadcasted_iota(jnp.int32, (size, 128), 1)
        first = jnp.where(empty & (lane == 0), MARK, rows[:, :128])
        packed = jnp.concatenate([first, rows[:, 128:]], axis=1).astype(jnp.bfloat16)
        if k == 0:
            blk_b[pl.ds(0, GROUP), :] = packed[:GROUP]
            pack[pl.ds(GROUP, size - GROUP), :] = packed[GROUP:]
            pl.semaphore_wait(barrier, len(partners))
        else:
            pack[pl.ds(k * size, size), :] = packed
        for j in range(k * size // GROUP, (k + 1) * size // GROUP):
            if j == 0:
                spread(0, True).start()
                spread(0, False).start()
            else:
                send(j).start()

    for j in range(1, N_MSG):
        send(j).wait_recv()
        spread(j, True).start()
        spread(j, False).start()

    ones = jnp.where(lax.broadcasted_iota(jnp.int32, (16, 128), 1) == 0, 1.0, 0.0).astype(jnp.bfloat16)

    def lows(block, low):
        marks = nt(ones, block[:, :128])[0:1]
        low[...] = jnp.where(marks > 2.0, LOW, 0.0)

    def product(left, l0, left_max, right, r0, right_low, right_max, same=False):
        scores = nt(left[pl.ds(l0, HALF), :], right[pl.ds(r0, HALF), :])
        if same:
            at0 = lax.broadcasted_iota(jnp.int32, (HALF, HALF), 0)
            at1 = lax.broadcasted_iota(jnp.int32, (HALF, HALF), 1)
            scores = jnp.where(at0 == at1, LOW, scores)
        marks = left[pl.ds(l0, HALF), 0:1].astype(jnp.float32)
        scores = scores + jnp.where(marks > 2.0, LOW, 0.0)
        down_max = jnp.max(scores, axis=0, keepdims=True)
        q0 = r0 // 128
        for q in range(HALF // 128):
            right_max[q0 + q] = jnp.maximum(right_max[q0 + q], down_max[:, q * 128 : (q + 1) * 128])
        if left_max is not None:
            wide = scores + right_low[...][:, r0 : r0 + HALF] if isinstance(r0, int) else scores + low_half(right_low, r0)
            best = jnp.maximum(
                jnp.maximum(wide[:, 0:128], wide[:, 128:256]), jnp.maximum(wide[:, 256:384], wide[:, 384:512])
            )
            for q in range(HALF // 128):
                turned = best[q * 128 : (q + 1) * 128, :].T
                left_max[l0 // 128 + q] = jnp.maximum(
                    left_max[l0 // 128 + q], jnp.max(turned, axis=0, keepdims=True)
                )

    def low_half(low, r0):
        return jnp.where(r0 == 0, low[...][:, :HALF], low[...][:, HALF:])

    for ref in (max_b, max_a, max_c, max_e):
        ref[...] = jnp.full(ref.shape, LOW, jnp.float32)

    lows(blk_b, low_b)
    product(blk_b, 0, None, blk_b, 0, low_b, max_b, same=True)
    product(blk_b, HALF, None, blk_b, HALF, low_b, max_b, same=True)
    product(blk_b, 0, max_b, blk_b, HALF, low_b, max_b)

    for j in range(N_MSG):
        spread(j, False).wait_recv()
        relay(j).start()
    lows(blk_c, low_c)
    for l0 in (0, HALF):
        for r0 in (0, HALF):
            product(blk_b, l0, max_b, blk_c, r0, low_c, max_c)
    for j in range(N_MSG):
        spread(j, True).wait_recv()
    for k in range(2):
        product(blk_a, k * HALF, max_a, blk_c, (wrapped + k) % 2 * HALF, low_c, max_c)
    for j in range(N_MSG):
        relay(j).wait_recv()
    lows(blk_e, low_e)
    for l0 in (0, HALF):
        for r0 in (0, HALF):
            product(blk_b, l0, max_b, blk_e, r0, low_e, max_e)
    for k in range(2):
        product(blk_a, k * HALF, max_a, blk_e, (wrapped + k) % 2 * HALF, low_e, max_e)
        product(blk_c, k * HALF, max_c, blk_e, (odd + k) % 2 * HALF, low_e, max_e)

    parts = [
        pltpu.make_async_remote_copy(
            src_ref=ref, dst_ref=got.at[n], send_sem=part_send.at[n], recv_sem=part_recv.at[n],
            device_id=other, device_id_type=MESH,
        )
        for n, (ref, other) in enumerate(((max_a, down), (max_c, up), (max_e, up_across)))
    ]
    for copy in parts:
        copy.start()
    for copy in parts:
        copy.wait_recv()
    max_b[...] = jnp.maximum(jnp.maximum(max_b[...], got[0]), jnp.maximum(got[1], got[2]))

    replies = []
    for j, (s, d, f) in enumerate(ORDER):
        if j == 0:
            continue
        replies.append(
            pltpu.make_async_remote_copy(
                src_ref=max_b.at[d * 2 + f], dst_ref=table.at[j],
                send_sem=reply_send.at[j], recv_sem=reply_recv.at[j],
                device_id=routed(x, y, z, c, s, d, f, -1), device_id_type=MESH,
            )
        )
    for copy in replies:
        copy.start()
    table[0] = max_b[0]
    for copy in replies:
        copy.wait_recv()

    values = jnp.concatenate([table[j] for j in range(N_MSG)], axis=0)
    high = values.astype(jnp.bfloat16)
    rest = values - high.astype(jnp.float32)
    mid = rest.astype(jnp.bfloat16)
    last = (rest - mid.astype(jnp.float32)).astype(jnp.bfloat16)
    choose = mine_f.astype(jnp.bfloat16)

    def taken(v):
        return lax.dot_general(v, choose, (((0,), (0,)), ((), ())), preferred_element_type=jnp.float32)

    lanes = taken(high) + taken(mid) + taken(last)
    want = s_of * GROUP + rank
    at = lax.broadcasted_iota(jnp.int32, (128, count), 0)
    out_ref[...] = jnp.sum(jnp.where(at == want, lanes, 0.0), axis=0, keepdims=True)

    for j in range(N_MSG):
        if j:
            send(j).wait_send()
        spread(j, True).wait_send()
        spread(j, False).wait_send()
        relay(j).wait_send()
    for copy in parts + replies:
        copy.wait_send()


def on_device(embed, dest, slot):
    count = embed.shape[0]
    width = embed.shape[1]
    vmem = pl.BlockSpec(memory_space=pltpu.VMEM)
    block = pltpu.VMEM((ROWS, width), jnp.bfloat16)
    low = pltpu.VMEM((1, ROWS), jnp.float32)
    best = pltpu.VMEM((ROWS // 128, 1, 128), jnp.float32)
    dma = pltpu.SemaphoreType.DMA
    out = pl.pallas_call(
        kernel,
        out_shape=jax.ShapeDtypeStruct((1, count), jnp.float32),
        in_specs=[vmem, vmem],
        out_specs=vmem,
        scratch_shapes=[
            pltpu.VMEM((count, width), jnp.bfloat16), block, block, block, block, block, low, low, low, low,
            best, best, best, best,
            pltpu.VMEM((3, ROWS // 128, 1, 128), jnp.float32), pltpu.VMEM((N_MSG, 1, 128), jnp.float32),
        ]
        + [dma((N_MSG,))] * 8
        + [dma((3,)), dma((3,)), dma((N_MSG,)), dma((N_MSG,)), dma(())],
        compiler_params=pltpu.CompilerParams(
            collective_id=0, has_side_effects=True, vmem_limit_bytes=48 * 2**20
        ),
        cost_estimate=pl.CostEstimate(flops=11 * 10**9, bytes_accessed=2 * 2**20, transcendentals=512),
    )(embed, dest.reshape(1, count))
    return out.reshape(count)


def solution(mesh):
    placed = (P(("grp", "blk"), None), P(("grp", "blk")), P(("grp", "blk")))
    return jax.shard_map(
        on_device, mesh=mesh, in_specs=placed, out_specs=P(("grp", "blk")), check_vma=False
    )
```

time: 222 us -> 68.2 us (0.31)
  waiting for transfers between devices: 145 us -> 0 us
  Pallas kernels: 0 us -> 65.5 us
  starting transfers between devices: 23.3 us -> 0 us
  local copies, waits for them, and re-layouts: 25.4 us -> 2.49 us
  between operations: 13.5 us -> 0.01 us
  matrix products: 9.47 us -> 0 us
  other arithmetic: 4.57 us -> 0 us
    all_gather x1 -> x0, waiting for transfers between devices: 105 us -> none  [on_device(): piece = lax.all_gather(unit, 'blk', axis=0, tiled=True)]
    pallas_call x0 -> x1, Pallas kernels: none -> 65.5 us  [on_device(): pl.pallas_call(kernel, out_shape=jax.ShapeDtypeStruct((1, count), jnp.flo...]
    all_to_all x3 -> x0, waiting for transfers between devices: 40.8 us -> none  [the longest x1 27 us: on_device(): lax.all_to_all(send_rows, ('grp', 'blk'), split_axis=0, concat_axis=0, ti...]
    all_to_all x3 -> x0, starting transfers between devices: 23.2 us -> none  [the longest x1 11.5 us: on_device(): lax.all_to_all(send_slots, ('grp', 'blk'), split_axis=0, concat_axis=0, t...]
    scatter x3 -> x0, local copies, waits for them, and re-layouts: 13.1 us -> none  [the longest x1 5.67 us: on_device(): members = jnp.zeros((count, width), jnp.bfloat16).at[arrived_slots].set(a...]
    gather x3 -> x0, local copies, waits for them, and re-layouts: 10.4 us -> none  [the longest x2 6.94 us: on_device(): best_member.at[arrived_slots].get(mode='fill', fill_value=0.0)]
    dot_general x2 -> x0, matrix products: 9.47 us -> none  [the longest x1 8.41 us: tile_scores(): lax.dot_general(left, right, (((1,), (1,)), ((), ())), preferred_element_...]
    unnamed x0 -> x5, local copies, waits for them, and re-layouts: none -> 2.49 us
  transfers between devices with their start and end apart: 4 -> 0, of which waited for: 4 -> 0; matrix products, arithmetic and copies ran while one was open for 3% -> 0% of each run, Pallas kernels for 0% -> 0%
where the time goes in v1:
time: 68.2 us; the launch traced here: 68 us
  Pallas kernels  65.5 us (96%)
  local copies, waits for them, and re-layouts  2.49 us (4%)
    pallas_call x1, Pallas kernels, on_device(): pl.pallas_call(kernel, out_shape=jax.ShapeDtypeStruct((1, count), jnp.flo...  65.5 us
    unnamed x5, local copies, waits for them, and re-layouts  2.49 us

profile of v1, /device:TPU:1, one launch (start us, length us, event | category | flops | bytes accessed | tf_op | source)
XLA Modules:
  0.0 68.0 jit_solution(13114079153916951521)
XLA Ops:
  0.0 0.0 copy-start
  0.0 1.2 %copy-done = bf16[512,1024]{1,0:T(8,128)(2,1)S(1)} copy-done((bf16[512,1024]{1,0:T(8,128)(2,1)S(1)}, bf16[512,1024]{1,0:T(8,128)(2,1)}, u32[]{:S(2)}) %copy-start) | copy-done | bytes 1048600
  1.2 0.0 copy-start.1
  1.2 0.7 copy-done.1
  1.9 65.5 %shard_map.28 = f32[1,512]{1,0:T(1,128)S(1)} custom-call(bf16[512,1024]{1,0:T(8,128)(2,1)S(1)} %copy-done, s32[1,512]{1,0:T(1,128)S(1)} %bitcast.3), custom_call_target="tpu_custom_call" | custom-call | flops 11000000512 | bytes 2097152 | tf_op jit(solution)/shard_map/pallas_call | solution.py:305
  67.4 0.6 copy.4
Async XLA Ops:
  0.0 1.2 %copy-start = (bf16[512,1024]{1,0:T(8,128)(2,1)S(1)}, bf16[512,1024]{1,0:T(8,128)(2,1)}, u32[]{:S(2)}) copy-start(bf16[512,1024]{1,0:T(8,128)(2,1)} %embed_ref.1) | copy-start | bytes 3145732
  1.2 0.7 %copy-start.1 = (s32[512]{0:T(512)S(1)}, s32[512]{0:T(512)}, u32[]{:S(2)}) copy-start(s32[512]{0:T(512)} %param.4) | copy-start | bytes 6148

commit v2 on v1

v2 whole, which is shorter than its diff:
```python
import jax
import jax.numpy as jnp
from jax import lax
from jax.experimental import pallas as pl
from jax.experimental.pallas import tpu as pltpu
from jax.sharding import PartitionSpec as P

MESH = pl.DeviceIdType.MESH
LAG = 4
GROUP = 64
N_MSG = 16
ROWS = GROUP * N_MSG
PIECE = 256
MARK = 4.0
LOW = -8.0

ORDER = [
    (0, 0, 0), (1, 0, 0), (0, 1, 0), (1, 1, 0), (0, 3, 0), (1, 3, 0), (0, 0, 1), (1, 0, 1),
    (0, 2, 0), (1, 2, 0), (0, 1, 1), (1, 1, 1), (0, 3, 1), (1, 3, 1), (0, 2, 1), (1, 2, 1),
]


def place():
    g = lax.axis_index("grp")
    b = lax.axis_index("blk")
    x = ((b >> 2) << 1) + (g >> 3)
    return x, (g >> 1) & 3, b & 3, g & 1


def device(x, y, z, c):
    return (((x & 1) << 3) + (y << 1) + c, ((x >> 1) << 2) + z)


def flip(y, kind):
    return jnp.where(kind == 0, 3 - y, y + 1 - 2 * (y & 1))


def mate(y, kind):
    return flip(y, 1 - kind)


def routed(x, y, z, c, s, d, f, sign):
    here = c if s == 0 else 1 - c
    kind = here if sign == 1 else c
    step = sign * d
    yy = flip(y, kind) if f else y
    xx = jnp.where(kind == 0, (x + step) & 3, x)
    zz = jnp.where(kind == 0, z, (z + step) & 3)
    return device(xx, yy, zz, here)


def ring(x, y, z, c, step, paired):
    yy = mate(y, c) if paired else y
    xx = jnp.where(c == 0, x, (x + step) & 3)
    zz = jnp.where(c == 0, (z + step) & 3, z)
    return device(xx, yy, zz, c)


def nt(a, b):
    return lax.dot_general(a, b, (((1,), (1,)), ((), ())), preferred_element_type=jnp.float32)


def kernel(
    embed_hbm, dest_hbm, out_ref,
    embed_ref, dest_ref, load_sem, unit, pack, blk_b, blk_a, blk_c, blk_e, low_b, low_a, low_c, low_e,
    max_b, max_a, max_c, max_e, got, table,
    pack_send, pack_recv, up_send, up_recv, down_send, down_recv, pair_send, pair_recv,
    part_send, part_recv, reply_send, reply_recv,
):
    x, y, z, c = place()
    embed_in = pltpu.make_async_copy(embed_hbm, embed_ref, load_sem.at[0])
    dest_in = pltpu.make_async_copy(dest_hbm, dest_ref, load_sem.at[1])
    dest_in.start()
    embed_in.start()

    barrier = pltpu.get_barrier_semaphore()
    partners = []
    for s, d, f in ORDER[1:]:
        partners.append(routed(x, y, z, c, s, d, f, -1))
    for s, d, f in ORDER[1:]:
        if s == 1 and (d, f) != (0, 0):
            partners.append(routed(x, y, z, c, s, d, f, 1))
    up = ring(x, y, z, c, 1, False)
    down = ring(x, y, z, c, 3, False)
    across = ring(x, y, z, c, 0, True)
    up_across = ring(x, y, z, c, 1, True)
    down_across = ring(x, y, z, c, 3, True)
    partners += [up, down, across, down_across]
    for other in partners:
        pl.semaphore_signal(barrier, inc=1, device_id=other, device_id_type=MESH)

    dest_in.wait()
    dest = dest_ref[...]
    count = dest.shape[1]
    cluster = dest >> 3
    kind = cluster >> 3
    ring_at = (cluster >> 1) & 3
    pair_at = cluster & 1
    s_of = jnp.where(kind == c, 0, 1)
    d_of = (jnp.where(kind == 0, ring_at - x, ring_at - z)) & 3
    my_pair0 = y >> 1
    my_pair1 = ((y + 1) & 3) >> 1
    f_of = jnp.where(jnp.where(kind == 0, my_pair0, my_pair1) == pair_at, 0, 1)
    code = (d_of * 2 + f_of) * 2 + s_of
    message = jnp.zeros_like(code)
    for j, (s, d, f) in enumerate(ORDER):
        message = jnp.where(code == (d * 2 + f) * 2 + s, j, message)
    mine = lax.broadcasted_iota(jnp.int32, (N_MSG, count), 0) == message
    earlier = (
        lax.broadcasted_iota(jnp.int32, (count, count), 0)
        < lax.broadcasted_iota(jnp.int32, (count, count), 1)
    ).astype(jnp.float32).astype(jnp.bfloat16)
    mine_f = mine.astype(jnp.float32)
    before = jnp.dot(mine_f.astype(jnp.bfloat16), earlier, preferred_element_type=jnp.float32)
    rank = jnp.sum(before * mine_f, axis=0, keepdims=True).astype(jnp.int32)
    position = message * GROUP + rank

    embed_in.wait()
    wide = embed_ref[...].astype(jnp.float32)
    scale = lax.rsqrt(jnp.sum(wide * wide, axis=1, keepdims=True) + 1e-06)
    unit[...] = (wide * scale).astype(jnp.bfloat16)


    def send(j):
        s, d, f = ORDER[j]
        rows = pl.ds(j * GROUP, GROUP)
        return pltpu.make_async_remote_copy(
            src_ref=pack.at[pl.ds(j * GROUP, GROUP)], dst_ref=blk_b.at[rows],
            send_sem=pack_send.at[j], recv_sem=pack_recv.at[j],
            device_id=routed(x, y, z, c, s, d, f, 1), device_id_type=MESH,
        )

    def spread(j, upward):
        rows = pl.ds(j * GROUP, GROUP)
        return pltpu.make_async_remote_copy(
            src_ref=blk_b.at[rows], dst_ref=(blk_a if upward else blk_c).at[rows],
            send_sem=(up_send if upward else down_send).at[j],
            recv_sem=(up_recv if upward else down_recv).at[j],
            device_id=up if upward else down, device_id_type=MESH,
        )

    def relay(j):
        rows = pl.ds(j * GROUP, GROUP)
        return pltpu.make_async_remote_copy(
            src_ref=blk_c.at[rows], dst_ref=blk_e.at[rows],
            send_sem=pair_send.at[j], recv_sem=pair_recv.at[j],
            device_id=across, device_id_type=MESH,
        )

    part = 4
    size = ROWS // part
    for k in range(part):
        at = lax.broadcasted_iota(jnp.int32, (size, count), 0) + k * size
        pick = (at == position).astype(jnp.float32)
        rows = jnp.dot(pick.astype(jnp.bfloat16), unit[...], preferred_element_type=jnp.float32)
        empty = jnp.sum(pick, axis=1, keepdims=True) < 0.5
        lane = lax.broadcasted_iota(jnp.int32, (size, 128), 1)
        first = jnp.where(empty & (lane == 0), MARK, rows[:, :128])
        packed = jnp.concatenate([first, rows[:, 128:]], axis=1).astype(jnp.bfloat16)
        if k == 0:
            blk_b[pl.ds(0, GROUP), :] = packed[:GROUP]
            pack[pl.ds(GROUP, size - GROUP), :] = packed[GROUP:]
            pl.semaphore_wait(barrier, len(partners))
        else:
            pack[pl.ds(k * size, size), :] = packed
        for j in range(k * size // GROUP, (k + 1) * size // GROUP):
            if j == 0:
                spread(0, True).start()
                spread(0, False).start()
            else:
                send(j).start()

    ones = jnp.where(lax.broadcasted_iota(jnp.int32, (16, 128), 1) == 0, 1.0, 0.0).astype(jnp.bfloat16)
    blocks = {"a": (blk_a, low_a, max_a), "b": (blk_b, low_b, max_b), "c": (blk_c, low_c, max_c), "e": (blk_e, low_e, max_e)}
    here = {name: [] for name in blocks}

    def meets(one, i, two, j):
        if one == two:
            return one == "b"
        if "b" in (one, two):
            return "a" not in (one, two)
        if one == "e" or (one == "a" and two == "c"):
            i, j = j, i
        return i >= j

    def compare(name, q):
        block, low, left_max = blocks[name]
        rows = block[pl.ds(q * PIECE, PIECE), :]
        marks = nt(ones, rows[:, :128])[0:1]
        low[:, pl.ds(q * PIECE, PIECE)] = jnp.where(marks > 2.0, LOW, 0.0)
        here[name].append(q)
        spans = []
        for other in blocks:
            run = None
            for k in range(ROWS // PIECE + 1):
                if k in here[other] and meets(name, q, other, k):
                    run = k if run is None else run
                elif run is not None:
                    spans.append((other, run * PIECE, (k - run) * PIECE))
                    run = None
        if not spans:
            return
        tilt = jnp.where(rows[:, 0:1].astype(jnp.float32) > 2.0, LOW, 0.0)
        best = None
        for other, start, width in spans:
            right, right_low, right_max = blocks[other]
            scores = nt(rows, right[pl.ds(start, width), :]) + tilt
            if other == name:
                at0 = lax.broadcasted_iota(jnp.int32, scores.shape, 0) + q * PIECE
                at1 = lax.broadcasted_iota(jnp.int32, scores.shape, 1) + start
                scores = jnp.where(at0 == at1, LOW, scores)
            tops = jnp.max(scores, axis=0, keepdims=True)
            for n in range(width // 128):
                at = start // 128 + n
                right_max[at] = jnp.maximum(right_max[at], tops[:, n * 128 : (n + 1) * 128])
            scores = scores + right_low[:, pl.ds(start, width)]
            for n in range(width // 128):
                tile = scores[:, n * 128 : (n + 1) * 128]
                best = tile if best is None else jnp.maximum(best, tile)
        for n in range(PIECE // 128):
            turned = best[n * 128 : (n + 1) * 128, :].T
            at = q * (PIECE // 128) + n
            left_max[at] = jnp.maximum(left_max[at], jnp.max(turned, axis=0, keepdims=True))

    per = PIECE // GROUP
    last = ROWS // PIECE - 1

    def of_piece(q):
        return range(q * per, (q + 1) * per)

    def compare_e(q):
        for j in of_piece(q):
            relay(j).wait_recv()
        compare("e", q)

    def passed(j):
        spread(j, False).wait_recv()
        relay(j).start()
        if j % per == per - 1:
            q = j // per
            compare("c", q)
            for k in of_piece(q):
                spread(k, True).wait_recv()
            compare("a", q)
        if j % per == 1 and j > per:
            compare_e(j // per - 1)

    for ref in (max_b, max_a, max_c, max_e):
        ref[...] = jnp.full(ref.shape, LOW, jnp.float32)
    for j in range(N_MSG):
        if j:
            send(j).wait_recv()
            spread(j, True).start()
            spread(j, False).start()
        if j >= LAG:
            passed(j - LAG)
        if j % per == per - 1:
            compare("b", j // per)
    for j in range(N_MSG - LAG, N_MSG):
        passed(j)
    compare_e(last)

    parts = [
        pltpu.make_async_remote_copy(
            src_ref=ref, dst_ref=got.at[n], send_sem=part_send.at[n], recv_sem=part_recv.at[n],
            device_id=other, device_id_type=MESH,
        )
        for n, (ref, other) in enumerate(((max_a, down), (max_c, up), (max_e, up_across)))
    ]
    for copy in parts:
        copy.start()
    for copy in parts:
        copy.wait_recv()
    max_b[...] = jnp.maximum(jnp.maximum(max_b[...], got[0]), jnp.maximum(got[1], got[2]))

    replies = []
    for j, (s, d, f) in enumerate(ORDER):
        if j == 0:
            continue
        replies.append(
            pltpu.make_async_remote_copy(
                src_ref=max_b.at[j // 2], dst_ref=table.at[j],
                send_sem=reply_send.at[j], recv_sem=reply_recv.at[j],
                device_id=routed(x, y, z, c, s, d, f, -1), device_id_type=MESH,
            )
        )
    for copy in replies:
        copy.start()
    table[0] = max_b[0]
    for copy in replies:
        copy.wait_recv()

    values = jnp.concatenate([table[j] for j in range(N_MSG)], axis=0)
    high = values.astype(jnp.bfloat16)
    rest = values - high.astype(jnp.float32)
    mid = rest.astype(jnp.bfloat16)
    last = (rest - mid.astype(jnp.float32)).astype(jnp.bfloat16)
    choose = mine_f.astype(jnp.bfloat16)

    def taken(v):
        return lax.dot_general(v, choose, (((0,), (0,)), ((), ())), preferred_element_type=jnp.float32)

    lanes = taken(high) + taken(mid) + taken(last)
    want = (message & 1) * GROUP + rank
    at = lax.broadcasted_iota(jnp.int32, (128, count), 0)
    out_ref[...] = jnp.sum(jnp.where(at == want, lanes, 0.0), axis=0, keepdims=True)

    for j in range(N_MSG):
        if j:
            send(j).wait_send()
        spread(j, True).wait_send()
        spread(j, False).wait_send()
        relay(j).wait_send()
    for copy in parts + replies:
        copy.wait_send()


def on_device(embed, dest, slot):
    count = embed.shape[0]
    width = embed.shape[1]
    vmem = pl.BlockSpec(memory_space=pltpu.VMEM)
    block = pltpu.VMEM((ROWS, width), jnp.bfloat16)
    low = pltpu.VMEM((1, ROWS), jnp.float32)
    best = pltpu.VMEM((ROWS // 128, 1, 128), jnp.float32)
    dma = pltpu.SemaphoreType.DMA
    out = pl.pallas_call(
        kernel,
        out_shape=jax.ShapeDtypeStruct((1, count), jnp.float32),
        in_specs=[pl.BlockSpec(memory_space=pl.ANY)] * 2,
        out_specs=vmem,
        scratch_shapes=[
            pltpu.VMEM((count, width), jnp.bfloat16), pltpu.VMEM((1, count), jnp.int32), dma((2,)),
            pltpu.VMEM((count, width), jnp.bfloat16), block, block, block, block, block, low, low, low, low,
            best, best, best, best,
            pltpu.VMEM((3, ROWS // 128, 1, 128), jnp.float32), pltpu.VMEM((N_MSG, 1, 128), jnp.float32),
        ]
        + [dma((N_MSG,))] * 8
        + [dma((3,)), dma((3,)), dma((N_MSG,)), dma((N_MSG,))],
        compiler_params=pltpu.CompilerParams(
            collective_id=0, has_side_effects=True, vmem_limit_bytes=60 * 2**20
        ),
        cost_estimate=pl.CostEstimate(flops=11 * 10**9, bytes_accessed=2 * 2**20, transcendentals=512),
    )(embed, dest.reshape(1, count))
    return out.reshape(count)


def solution(mesh):
    placed = (P(("grp", "blk"), None), P(("grp", "blk")), P(("grp", "blk")))
    return jax.shard_map(
        on_device, mesh=mesh, in_specs=placed, out_specs=P(("grp", "blk")), check_vma=False
    )
```

time: 68.2 us -> 64.1 us (0.940)
  Pallas kernels: 65.5 us -> 62.7 us
  local copies, waits for them, and re-layouts: 2.49 us -> 1.26 us
    pallas_call x1, Pallas kernels: 65.5 us -> 62.7 us  [on_device(): pl.pallas_call(kernel, out_shape=jax.ShapeDtypeStruct((1, count), jnp.flo...]
    unnamed x5 -> x1, local copies, waits for them, and re-layouts: 2.49 us -> 1.26 us
where the time goes in v2:
time: 64.1 us; the launch traced here: 63.9 us
  Pallas kernels  62.7 us (98%)
  local copies, waits for them, and re-layouts  1.26 us (2%)
    pallas_call x1, Pallas kernels, on_device(): pl.pallas_call(kernel, out_shape=jax.ShapeDtypeStruct((1, count), jnp.flo...  62.7 us

profile of v2, /device:TPU:1, one launch (start us, length us, event | category | flops | bytes accessed | tf_op | source)
XLA Modules:
  0.0 63.9 jit_solution(5810501719340001399)
XLA Ops:
  0.0 62.7 %shard_map.28 = f32[1,512]{1,0:T(1,128)} custom-call(bf16[512,1024]{1,0:T(8,128)(2,1)} %embed_hbm.1, s32[1,512]{1,0:T(1,128)} %bitcast.3), custom_call_target="tpu_custom_call" | custom-call | flops 11000000512 | bytes 2097152 | tf_op jit(solution)/shard_map/pallas_call | solution.py:326
  62.7 1.3 %copy.4 = f32[512]{0:T(512)} copy(f32[512]{0:T(512)} %bitcast.2) | data formatting | bytes 4096

commit v3 on v2

--- a/solution.py
+++ b/solution.py
@@ -1,3 +1,5 @@
+import functools
+
 import jax
 import jax.numpy as jnp
 from jax import lax
@@ -6,6 +8,8 @@
 from jax.sharding import PartitionSpec as P
 
 MESH = pl.DeviceIdType.MESH
+BUDGET = 1024
+LATER = 2
 LAG = 4
 GROUP = 64
 N_MSG = 16
@@ -20,6 +24,10 @@
 ]
 
 
+PER = PIECE // GROUP
+LATE = ORDER[N_MSG - PER :]
+
+
 def place():
     g = lax.axis_index("grp")
     b = lax.axis_index("blk")
@@ -40,20 +48,28 @@
 
 
 def routed(x, y, z, c, s, d, f, sign):
+    return device(*end_of(x, y, z, c, s, d, f, sign))
+
+
+def end_of(x, y, z, c, s, d, f, sign):
     here = c if s == 0 else 1 - c
     kind = here if sign == 1 else c
     step = sign * d
     yy = flip(y, kind) if f else y
     xx = jnp.where(kind == 0, (x + step) & 3, x)
     zz = jnp.where(kind == 0, z, (z + step) & 3)
-    return device(xx, yy, zz, here)
-
-
-def ring(x, y, z, c, step, paired):
+    return xx, yy, zz, here
+
+
+def moved(x, y, z, c, step, paired):
     yy = mate(y, c) if paired else y
     xx = jnp.where(c == 0, x, (x + step) & 3)
     zz = jnp.where(c == 0, (z + step) & 3, z)
-    return device(xx, yy, zz, c)
+    return xx, yy, zz, c
+
+
+def ring(x, y, z, c, step, paired):
+    return device(*moved(x, y, z, c, step, paired))
 
 
 def nt(a, b):
@@ -63,9 +79,9 @@
 def kernel(
     embed_hbm, dest_hbm, out_ref,
     embed_ref, dest_ref, load_sem, unit, pack, blk_b, blk_a, blk_c, blk_e, low_b, low_a, low_c, low_e,
-    max_b, max_a, max_c, max_e, got, table,
+    max_b, max_a, max_c, max_e, got, table, extra,
     pack_send, pack_recv, up_send, up_recv, down_send, down_recv, pair_send, pair_recv,
-    part_send, part_recv, reply_send, reply_recv,
+    part_send, part_recv, reply_send, reply_recv, answer_send, answer_recv,
 ):
     x, y, z, c = place()
     embed_in = pltpu.make_async_copy(embed_hbm, embed_ref, load_sem.at[0])
@@ -86,6 +102,8 @@
     up_across = ring(x, y, z, c, 1, True)
     down_across = ring(x, y, z, c, 3, True)
     partners += [up, down, across, down_across]
+    for s, d, f in LATE:
+        partners.append(ring(*end_of(x, y, z, c, s, d, f, 1), 3, True))
     for other in partners:
         pl.semaphore_signal(barrier, inc=1, device_id=other, device_id_type=MESH)
 
@@ -171,7 +189,7 @@
                 send(j).start()
 
     ones = jnp.where(lax.broadcasted_iota(jnp.int32, (16, 128), 1) == 0, 1.0, 0.0).astype(jnp.bfloat16)
-    blocks = {"a": (blk_a, low_a, max_a), "b": (blk_b, low_b, max_b), "c": (blk_c, low_c, max_c), "e": (blk_e, low_e, max_e)}
+    blocks = {"a": (blk_a, low_a, max_a), "c": (blk_c, low_c, max_c), "e": (blk_e, low_e, max_e), "b": (blk_b, low_b, max_b)}
     here = {name: [] for name in blocks}
 
     def meets(one, i, two, j):
@@ -192,86 +210,120 @@
         spans = []
         for other in blocks:
             run = None
+            once = name == "e" and other in ("a", "c")
+            if once:
+                spans.append((other, q * PIECE, PIECE))
             for k in range(ROWS // PIECE + 1):
-                if k in here[other] and meets(name, q, other, k):
+                if k in here[other] and meets(name, q, other, k) and not (once and k == q):
                     run = k if run is None else run
                 elif run is not None:
                     spans.append((other, run * PIECE, (k - run) * PIECE))
                     run = None
-        if not spans:
-            return
+        for other, start, width in spans:
+            for at in range(start, start + width, 2 * PIECE):
+                wide = min(2 * PIECE, start + width - at)
+                waiting.append((wide, functools.partial(product, name, q, other, at, wide)))
+
+    def product(name, q, other, start, width):
+        block, low, left_max = blocks[name]
+        right, right_low, right_max = blocks[other]
+        rows = block[pl.ds(q * PIECE, PIECE), :]
         tilt = jnp.where(rows[:, 0:1].astype(jnp.float32) > 2.0, LOW, 0.0)
-        best = None
-        for other, start, width in spans:
-            right, right_low, right_max = blocks[other]
-            scores = nt(rows, right[pl.ds(start, width), :]) + tilt
-            if other == name:
-                at0 = lax.broadcasted_iota(jnp.int32, scores.shape, 0) + q * PIECE
-                at1 = lax.broadcasted_iota(jnp.int32, scores.shape, 1) + start
-                scores = jnp.where(at0 == at1, LOW, scores)
+        scores = nt(rows, right[pl.ds(start, width), :]) + tilt
+        if other == name:
+            at0 = lax.broadcasted_iota(jnp.int32, scores.shape, 0) + q * PIECE
+            at1 = lax.broadcasted_iota(jnp.int32, scores.shape, 1) + start
+            scores = jnp.where(at0 == at1, LOW, scores)
+        if not (name == "e" and other in ("a", "c") and start == q * PIECE):
             tops = jnp.max(scores, axis=0, keepdims=True)
             for n in range(width // 128):
                 at = start // 128 + n
                 right_max[at] = jnp.maximum(right_max[at], tops[:, n * 128 : (n + 1) * 128])
-            scores = scores + right_low[:, pl.ds(start, width)]
-            for n in range(width // 128):
-                tile = scores[:, n * 128 : (n + 1) * 128]
-                best = tile if best is None else jnp.maximum(best, tile)
+        scores = scores + right_low[:, pl.ds(start, width)]
+        best = None
+        for n in range(width // 128):
+            tile = scores[:, n * 128 : (n + 1) * 128]
+            best = tile if best is None else jnp.maximum(best, tile)
         for n in range(PIECE // 128):
             turned = best[n * 128 : (n + 1) * 128, :].T
             at = q * (PIECE // 128) + n
             left_max[at] = jnp.maximum(left_max[at], jnp.max(turned, axis=0, keepdims=True))
 
-    per = PIECE // GROUP
+    def work(budget):
+        while waiting and budget > 0:
+            wide, step = waiting.pop(0)
+            step()
+            budget -= wide
+
+    waiting = []
     last = ROWS // PIECE - 1
 
     def of_piece(q):
-        return range(q * per, (q + 1) * per)
+        return range(q * PER, (q + 1) * PER)
 
     def compare_e(q):
         for j in of_piece(q):
             relay(j).wait_recv()
         compare("e", q)
 
-    def passed(j):
-        spread(j, False).wait_recv()
-        relay(j).start()
-        if j % per == per - 1:
-            q = j // per
-            compare("c", q)
-            for k in of_piece(q):
-                spread(k, True).wait_recv()
-            compare("a", q)
-        if j % per == 1 and j > per:
-            compare_e(j // per - 1)
-
     for ref in (max_b, max_a, max_c, max_e):
         ref[...] = jnp.full(ref.shape, LOW, jnp.float32)
-    for j in range(N_MSG):
-        if j:
+    for step in range(N_MSG + LAG):
+        j, k = step, step - LAG
+        if 0 < j < N_MSG:
             send(j).wait_recv()
             spread(j, True).start()
             spread(j, False).start()
-        if j >= LAG:
-            passed(j - LAG)
-        if j % per == per - 1:
-            compare("b", j // per)
-    for j in range(N_MSG - LAG, N_MSG):
-        passed(j)
-    compare_e(last)
-
+        if k >= 0:
+            spread(k, False).wait_recv()
+            relay(k).start()
+        if j < N_MSG and j % PER == PER - 1:
+            compare("b", j // PER)
+        if k >= 0 and k % PER == PER - 1:
+            compare("c", k // PER)
+            for n in of_piece(k // PER):
+                spread(n, True).wait_recv()
+            compare("a", k // PER)
+        if k >= PER and (k - LATER) % PER == PER - 1 and (k - LATER) // PER < last:
+            compare_e((k - LATER) // PER)
+        if step < N_MSG + LAG - 1:
+            work(BUDGET)
+    work(ROWS * ROWS)
+
+    early = pl.ds(0, last * (PIECE // 128))
     parts = [
         pltpu.make_async_remote_copy(
-            src_ref=ref, dst_ref=got.at[n], send_sem=part_send.at[n], recv_sem=part_recv.at[n],
+            src_ref=ref, dst_ref=dst, send_sem=part_send.at[n], recv_sem=part_recv.at[n],
             device_id=other, device_id_type=MESH,
         )
-        for n, (ref, other) in enumerate(((max_a, down), (max_c, up), (max_e, up_across)))
+        for n, (ref, dst, other) in enumerate(
+            (
+                (max_a, got.at[0], down),
+                (max_c, got.at[1], up),
+                (max_e.at[early], got.at[2, early], up_across),
+            )
+        )
     ]
     for copy in parts:
         copy.start()
+    compare_e(last)
+    work(ROWS * ROWS)
+    answers = []
+    for n, (s, d, f) in enumerate(LATE):
+        answers.append(
+            pltpu.make_async_remote_copy(
+                src_ref=max_e.at[(N_MSG - PER + n) // 2], dst_ref=extra.at[n],
+                send_sem=answer_send.at[n], recv_sem=answer_recv.at[n],
+                device_id=routed(*moved(x, y, z, c, 1, True), s, d, f, -1), device_id_type=MESH,
+            )
+        )
+    for copy in answers:
+        copy.start()
     for copy in parts:
         copy.wait_recv()
-    max_b[...] = jnp.maximum(jnp.maximum(max_b[...], got[0]), jnp.maximum(got[1], got[2]))
+    for n in range(ROWS // 128):
+        best = jnp.maximum(max_b[n], jnp.maximum(got[0, n], got[1, n]))
+        max_b[n] = jnp.maximum(best, got[2, n]) if n < last * (PIECE // 128) else best
 
     replies = []
     for j, (s, d, f) in enumerate(ORDER):
@@ -287,10 +339,12 @@
     for copy in replies:
         copy.start()
     table[0] = max_b[0]
-    for copy in replies:
+    for copy in answers + replies:
         copy.wait_recv()
 
-    values = jnp.concatenate([table[j] for j in range(N_MSG)], axis=0)
+    values = jnp.concatenate(
+        [table[j] if j < N_MSG - PER else jnp.maximum(table[j], extra[j - N_MSG + PER]) for j in range(N_MSG)], axis=0
+    )
     high = values.astype(jnp.bfloat16)
     rest = values - high.astype(jnp.float32)
     mid = rest.astype(jnp.bfloat16)
@@ -311,7 +365,7 @@
         spread(j, True).wait_send()
         spread(j, False).wait_send()
         relay(j).wait_send()
-    for copy in parts + replies:
+    for copy in parts + answers + replies:
         copy.wait_send()
 
 
@@ -333,9 +387,10 @@
             pltpu.VMEM((count, width), jnp.bfloat16), block, block, block, block, block, low, low, low, low,
             best, best, best, best,
             pltpu.VMEM((3, ROWS // 128, 1, 128), jnp.float32), pltpu.VMEM((N_MSG, 1, 128), jnp.float32),
+            pltpu.VMEM((PER, 1, 128), jnp.float32),
         ]
         + [dma((N_MSG,))] * 8
-        + [dma((3,)), dma((3,)), dma((N_MSG,)), dma((N_MSG,))],
+        + [dma((3,)), dma((3,)), dma((N_MSG,)), dma((N_MSG,)), dma((PER,)), dma((PER,))],
         compiler_params=pltpu.CompilerParams(
             collective_id=0, has_side_effects=True, vmem_limit_bytes=60 * 2**20
         ),

time: 64.1 us -> 62.2 us (0.970)
  Pallas kernels: 62.7 us -> 60.7 us
    pallas_call x1, Pallas kernels: 62.7 us -> 60.7 us  [on_device(): pl.pallas_call(kernel, out_shape=jax.ShapeDtypeStruct((1, count), jnp.flo...]
where the time goes in v3:
time: 62.2 us; the launch traced here: 62 us
  Pallas kernels  60.7 us (98%)
  local copies, waits for them, and re-layouts  1.26 us (2%)
    pallas_call x1, Pallas kernels, on_device(): pl.pallas_call(kernel, out_shape=jax.ShapeDtypeStruct((1, count), jnp.flo...  60.7 us
    unnamed x1, local copies, waits for them, and re-layouts  1.26 us

profile of v3, /device:TPU:1, one launch (start us, length us, event | category | flops | bytes accessed | tf_op | source)
XLA Modules:
  0.0 62.0 jit_solution(16601131392975665145)
XLA Ops:
  0.0 60.7 %shard_map.28 = f32[1,512]{1,0:T(1,128)} custom-call(bf16[512,1024]{1,0:T(8,128)(2,1)} %embed_hbm.1, s32[1,512]{1,0:T(1,128)} %bitcast.3), custom_call_target="tpu_custom_call" | custom-call | flops 11000000512 | bytes 2097152 | tf_op jit(solution)/shard_map/pallas_call | solution.py:380
  60.7 1.3 %copy.4 = f32[512]{0:T(512)} copy(f32[512]{0:T(512)} %bitcast.2) | data formatting | bytes 4096

commit v4 on v3

--- a/solution.py
+++ b/solution.py
@@ -379,7 +379,7 @@
     dma = pltpu.SemaphoreType.DMA
     out = pl.pallas_call(
         kernel,
-        out_shape=jax.ShapeDtypeStruct((1, count), jnp.float32),
+        out_shape=pltpu.VMEM((1, count), jnp.float32),
         in_specs=[pl.BlockSpec(memory_space=pl.ANY)] * 2,
         out_specs=vmem,
         scratch_shapes=[

time: 62.2 us -> 60.9 us (0.979)
  local copies, waits for them, and re-layouts: 1.26 us -> 0.58 us
    unnamed x1, local copies, waits for them, and re-layouts: 1.26 us -> 0.58 us
where the time goes in v4:
time: 60.9 us; the launch traced here: 60.7 us
  Pallas kernels  60.1 us (99%)
    pallas_call x1, Pallas kernels, on_device(): pl.pallas_call(kernel, out_shape=pltpu.VMEM((1, count), jnp.float32), in_...  60.1 us

profile of v4, /device:TPU:1, one launch (start us, length us, event | category | flops | bytes accessed | tf_op | source)
XLA Modules:
  0.0 60.7 jit_solution(12958063312232185084)
XLA Ops:
  0.0 60.1 %shard_map.28 = f32[1,512]{1,0:T(1,128)S(1)} custom-call(bf16[512,1024]{1,0:T(8,128)(2,1)} %embed_hbm.1, s32[1,512]{1,0:T(1,128)} %bitcast.3), custom_call_target="tpu_custom_call" | custom-call | flops 11000000512 | bytes 2097152 | tf_op jit(solution)/shard_map/pallas_call | solution.py:380
  60.1 0.6 copy.4

commit v5 on v4

--- a/solution.py
+++ b/solution.py
@@ -9,7 +9,7 @@
 
 MESH = pl.DeviceIdType.MESH
 BUDGET = 1024
-LATER = 2
+LATER = 3
 LAG = 4
 GROUP = 64
 N_MSG = 16

time: 60.9 us -> 59.4 us (0.975)
  Pallas kernels: 60.1 us -> 58.7 us
    pallas_call x1, Pallas kernels: 60.1 us -> 58.7 us  [on_device(): pl.pallas_call(kernel, out_shape=pltpu.VMEM((1, count), jnp.float32), in_...]
where the time goes in v5:
time: 59.4 us; the launch traced here: 59.3 us
  Pallas kernels  58.7 us (99%)
    pallas_call x1, Pallas kernels, on_device(): pl.pallas_call(kernel, out_shape=pltpu.VMEM((1, count), jnp.float32), in_...  58.7 us

profile of v5, /device:TPU:1, one launch (start us, length us, event | category | flops | bytes accessed | tf_op | source)
XLA Modules:
  0.0 59.3 jit_solution(12734671985765685762)
XLA Ops:
  0.0 58.7 %shard_map.28 = f32[1,512]{1,0:T(1,128)S(1)} custom-call(bf16[512,1024]{1,0:T(8,128)(2,1)} %embed_hbm.1, s32[1,512]{1,0:T(1,128)} %bitcast.3), custom_call_target="tpu_custom_call" | custom-call | flops 11000000512 | bytes 2097152 | tf_op jit(solution)/shard_map/pallas_call | solution.py:380
  58.7 0.6 copy.4
